TPU v7x, 32 devices: a whole 2x2x4 slice. The times are simulated.
32 devices in a mesh: dp: 8 (over z, y), tensor: 4 (over x, core).
Axes of the slice: x: 2, y: 2, z: 4, core: 2. Of those that a mesh axis runs over, the one named last changes fastest.
Arguments:
- out_grad: bfloat16 [4096, 4096], P(('dp', 'tensor')), may hold values from -6 to 6
- attn_out: bfloat16 [4096, 4096], P('dp', 'tensor'), may hold values from -0.25 to 0.25
- o_weight: bfloat16 [4096, 4096], P('dp', 'tensor'), may hold values from -0.09375 to 0.09375
Outputs:
- attn_grad: bfloat16 [4096, 4096], P('dp', 'tensor')
- weight_grad: float32 [4096, 4096], P('dp', 'tensor')
All inputs are finite; a program needn't handle non-finite values.
Results may differ from a plain program's by a relative error of at most 0.001.
Values may be sent and summed in bfloat16 or wider, within the bound.
A program may use at most 64 MiB of HBM per device.

v0:
```python
import jax
import jax.numpy as jnp
from jax import lax
from jax.sharding import PartitionSpec as P


def body(out_grad, attn_out, o_weight):
    full_weight = lax.all_gather(o_weight, "dp", axis=0, tiled=True)
    gathered = lax.all_gather(out_grad, "tensor", axis=0, tiled=True)
    attn_grad = jnp.dot(gathered, full_weight, preferred_element_type=jnp.float32).astype(
        jnp.bfloat16
    )
    weight_grad = lax.psum_scatter(
        lax.dot_general(
            gathered, attn_out, (((0,), (0,)), ((), ())), preferred_element_type=jnp.float32
        ),
        "dp",
        scatter_dimension=0,
        tiled=True,
    )
    return (attn_grad, weight_grad)


def solution(mesh):
    return jax.shard_map(
        body,
        mesh=mesh,
        in_specs=(P(("dp", "tensor"), None), P("dp", "tensor"), P("dp", "tensor")),
        out_specs=(P("dp", "tensor"), P("dp", "tensor")),
        check_vma=False,
    )
```

profile of v0, /device:TPU:0, one launch (start us, length us, event | category | flops | bytes accessed | tf_op | source)
XLA Modules:
  0.0 465.7 jit_solution(5538877359467617346)
XLA Ops:
  7.2 0.0 copy-start
  7.2 0.0 all-gather.3.cloned.1.call-start
  7.2 0.7 all-gather.3.cloned.1.call-update
  7.9 0.0 all-gather.5.cloned.1.call-start
  8.0 0.7 all-gather.5.cloned.1.call-update
  8.7 0.0 reduce-scatter.2.cloned.1.call-start
  8.7 38.1 %all-gather.3.cloned.1.call-done = bf16[512,4096]{1,0:T(8,128)(2,1)} async-done(((bf16[128,4096]{1,0:T(8,128)(2,1)}), bf16[512,4096]{1,0:T(8,128)(2,1)}) %all-gather.3.cloned.1.call-update) | async-done | bytes 4194320 | tf_op jit(solution)/shard_map/all_gather | solution.py:9
  46.8 0.0 copy-done
  46.8 10.6 %fusion = f32[4096,1024]{1,0:T(8,128)} fusion(bf16[512,4096]{1,0:T(8,128)(2,1)} %all-gather.3.cloned.1.call-done, bf16[512,1024]{1,0:T(8,128)(2,1)S(1)} %copy-done), kind=kOutput, calls=%fused_computation.1 | convolution fusion | flops 4294967296 | bytes 22020096 | tf_op jit(solution)/shard_map/dot_general | solution.py:14
  57.4 0.0 reduce-scatter.2.cloned.1.call-update
  57.4 116.5 %all-gather.5.cloned.1.call-done = bf16[4096,1024]{1,0:T(8,128)(2,1)} async-done(((bf16[512,1024]{1,0:T(8,128)(2,1)}), bf16[4096,1024]{1,0:T(8,128)(2,1)}) %all-gather.5.cloned.1.call-update) | async-done | bytes 8388624 | tf_op jit(solution)/shard_map/all_gather | solution.py:8
  173.9 10.1 %convolution_convert_fusion = bf16[512,1024]{1,0:T(8,128)(2,1)} fusion(bf16[512,4096]{1,0:T(8,128)(2,1)} %all-gather.3.cloned.1.call-done, bf16[4096,1024]{1,0:T(8,128)(2,1)} %all-gather.5.cloned.1.call-done), kind=kOutput, calls=%fused_computation | convolution fusion | flops 4295491584 | bytes 13631488 | tf_op jit(solution)/shard_map/dot_general | solution.py:10
  184.0 275.2 %reduce-scatter.2.cloned.1.call-done = f32[512,1024]{1,0:T(8,128)} async-done(((f32[4096,1024]{1,0:T(8,128)}), f32[512,1024]{1,0:T(8,128)}) %reduce-scatter.2.cloned.1.call-update) | async-done | bytes 2097168 | tf_op jit(solution)/shard_map/reduce_scatter | solution.py:13
Async XLA Ops:
  7.2 39.6 %copy-start = (bf16[512,1024]{1,0:T(8,128)(2,1)S(1)}, bf16[512,1024]{1,0:T(8,128)(2,1)}, u32[]{:S(2)}) copy-start(bf16[512,1024]{1,0:T(8,128)(2,1)} %param.4) | copy-start | bytes 3145732
  7.2 39.6 %all-gather.3.cloned.1.call-start = ((), (), s32[]{:S(2)}) async-start(), calls=%async_computation.1 | async-start | bytes 5242880 | tf_op jit(solution)/shard_map/all_gather | solution.py:9
  7.9 166.0 %all-gather.5.cloned.1.call-start = ((), (), s32[]{:S(2)}) async-start(), calls=%async_computation.2 | async-start | bytes 9437184 | tf_op jit(solution)/shard_map/all_gather | solution.py:8
  8.7 450.5 %reduce-scatter.2.cloned.1.call-start = ((), (), s32[]{:S(2)}) async-start(), calls=%async_computation.3 | async-start | bytes 18874368 | tf_op jit(solution)/shard_map/reduce_scatter | solution.py:13
Sparse Core Ops, SparseCore 0:
  9.6 37.1 all-gather.2
  48.9 124.9 all-gather.4
  178.2 280.9 reduce-scatter.1
where the time goes:
time: 466 us
  waiting for transfers between devices  431 us (92%)
  matrix products  20.7 us (4%)
  between operations  13.8 us (3%)
    reduce_scatter x1, waiting for transfers between devices, body(): lax.psum_scatter(lax.dot_general(gathered, attn_out, (((0,), (0,)), ((),...  275 us
    all_gather x1, waiting for transfers between devices, body(): full_weight = lax.all_gather(o_weight, 'dp', axis=0, tiled=True)  116 us
    all_gather x1, waiting for transfers between devices, body(): gathered = lax.all_gather(out_grad, 'tensor', axis=0, tiled=True)  38.1 us
    dot_general x1, matrix products, body(): lax.dot_general(gathered, attn_out, (((0,), (0,)), ((), ())), preferred_e...  10.6 us
    dot_general x1, matrix products, body(): jnp.dot(gathered, full_weight, preferred_element_type=jnp.float32)  10.1 us
  transfers between devices with their start and end apart: 3, of which 3 were waited for; matrix products, arithmetic and copies ran while one was open for 4% of the time, Pallas kernels for 0%

commit v1 on v0

v1 whole, which is shorter than its diff:
```python
import functools

import jax
import jax.numpy as jnp
from jax import lax
from jax.experimental import pallas as pl
from jax.experimental.pallas import tpu as pltpu
from jax.sharding import PartitionSpec as P

MESH = pl.DeviceIdType.MESH
CHUNK = 256


def kernel(n_dp, n_t, g_ref, a_ref, w_ref, attn_ref, wg_ref,
           G, A, W, up, down, acc, attn_send, attn_recv, wg_send, wg_recv,
           g_ssem, g_rsem, w_ssem, w_rsem, rs_ssem, rs_rsem, p_ssem, p_rsem):
    L, nx = n_dp // 2, n_t // 2
    T, S, R = g_ref.shape[0], a_ref.shape[0], w_ref.shape[0]
    H = a_ref.shape[1] // 2
    FB = 2 * R
    Q = FB // CHUNK
    K = 2 * S
    d, t = lax.axis_index("dp"), lax.axis_index("tensor")
    z, y = d // 2, d % 2
    x, c = t // 2, t % 2
    oy = 1 - y
    pair, core = (d + 1 - 2 * y, t), (d, t + 1 - 2 * c)
    above, below = (d + 2, t), (d - 2, t)
    has_above, has_below = z < L - 1, z > 0

    def beside(k):
        return (d, lax.rem(x + k, nx) * 2 + c)

    def cols(half):
        return pl.ds(pl.multiple_of(half * H, H), H)

    def copy(src, dst, ssem, rsem, to):
        return pltpu.make_async_remote_copy(
            src_ref=src, dst_ref=dst, send_sem=ssem, recv_sem=rsem, device_id=to, device_id_type=MESH)

    barrier = pltpu.get_barrier_semaphore()
    for other in [pair, core] + [beside(k) for k in range(1, nx)]:
        pl.semaphore_signal(barrier, inc=1, device_id=other, device_id_type=MESH)

    @pl.when(has_above)
    def _():
        pl.semaphore_signal(barrier, inc=1, device_id=above, device_id_type=MESH)

    @pl.when(has_below)
    def _():
        pl.semaphore_signal(barrier, inc=1, device_id=below, device_id_type=MESH)

    order = [v for s in range((L + 1) // 2) for v in ([L - 1 - s, s] if s != L - 1 - s else [s])]

    def block_at(p):
        return jnp.where(z < (L + 1) // 2, order[p], L - 1 - order[p])

    def g_slot(b, yy, xx, cc):
        row = pl.multiple_of((yy * n_t + xx * 2 + cc) * T, T)
        return G.at[b, pl.ds(row, T), :]

    def g_copy(p, slot, s_idx, r_idx, to):
        return copy(slot, slot, g_ssem.at[p, s_idx], g_rsem.at[p, r_idx], to)

    def xm(m):
        return lax.rem(x + m, nx)

    def g_own(p):
        b = block_at(p)
        slot = g_slot(b, y, x, c)
        slot[...] = g_ref[:, pl.ds(pl.multiple_of(b * FB, FB), FB)]
        g_copy(p, slot, 0, 0, pair).start()
        for k in range(1, nx):
            g_copy(p, slot, k, nx - k, beside(k)).start()
        g_copy(p, slot, 2 * nx - 1, 2 * nx - 1, core).start()

    def to_core(p, slot, j):
        g_copy(p, slot, 2 * nx - 1 + j, 2 * nx - 1 + j, core).start()

    def g_arrived(p, slot, r_idx):
        g_copy(p, slot, r_idx, r_idx, core).wait_recv()

    def g_from_pair(p):
        slot = g_slot(block_at(p), oy, x, c)
        g_arrived(p, slot, 0)
        for k in range(1, nx):
            g_copy(p, slot, nx - 1 + k, nx - 1 + nx - k, beside(k)).start()
        to_core(p, slot, nx)

    def g_rest(p):
        b = block_at(p)
        for m in range(1, nx):
            slot = g_slot(b, y, xm(m), c)
            g_arrived(p, slot, m)
            to_core(p, slot, m)
        for m in range(1, nx):
            slot = g_slot(b, oy, xm(m), c)
            g_arrived(p, slot, nx - 1 + m)
            to_core(p, slot, nx + m)
        for yy in range(2):
            for m in range(nx):
                slot = g_slot(b, y if yy == 0 else oy, xm(m), 1 - c)
                g_arrived(p, slot, 2 * nx - 1 + yy * nx + m)

    def g_sent(p):
        slot = g_slot(block_at(p), y, x, c)
        for i in range(4 * nx - 1):
            g_copy(p, slot, i, i, core).wait_send()

    def w_slot(b, yy):
        return W.at[b, pl.ds(pl.multiple_of(yy * R, R), R), :]

    def w_copy(b, yy, way, to):
        slot = w_slot(b, yy)
        return copy(slot, slot, w_ssem.at[way, b * 2 + yy], w_rsem.at[b * 2 + yy], to)

    def w_spread(b, yy, upward, downward):
        if upward:
            @pl.when(has_above)
            def _():
                w_copy(b, yy, 0, above).start()
        if downward:
            @pl.when(has_below)
            def _():
                w_copy(b, yy, 1, below).start()

    def a_swap(buf):
        return copy(a_ref.at[:, cols(oy)], buf.at[pl.ds(pl.multiple_of(y * S, S), S), :],
                    p_ssem.at[0], p_rsem.at[0], pair)

    def w_swap():
        return copy(w_ref.at[:, cols(oy)], w_slot(z, y), p_ssem.at[1], w_rsem.at[d], pair)

    def attn_block(b):
        def rows(i, _):
            r = pl.ds(pl.multiple_of(i * 256, 256), 256)
            acc[r, :] += jnp.dot(G[b, r, :], W[b], preferred_element_type=jnp.float32)
            return 0
        lax.fori_loop(0, K // 256, rows, 0)

    def w_wave(h):
        @pl.when(z - h >= 0)
        def _():
            for yy in range(2):
                w_copy(z - h, yy, 0, above).wait_recv()
                w_spread(z - h, yy, True, False)

        @pl.when(z + h <= L - 1)
        def _():
            for yy in range(2):
                w_copy(z + h, yy, 1, below).wait_recv()
                w_spread(z + h, yy, False, True)

        @pl.when(z - h >= 0)
        def _():
            attn_block(z - h)

        @pl.when(z + h <= L - 1)
        def _():
            attn_block(z + h)

    def rs_rows(q):
        return pl.ds(pl.multiple_of(q * CHUNK, CHUNK), CHUNK)

    def rs_copy(buf, way, b, q, to):
        slot = buf.at[b, rs_rows(q), :]
        return copy(slot, slot, rs_ssem.at[way, b, q], rs_rsem.at[way, b, q], to)

    def part(b, q):
        return lax.dot_general(G[b, :, rs_rows(q)], A[...], (((0,), (0,)), ((), ())),
                               preferred_element_type=jnp.float32)

    def rs_step(buf, way, b, q, has_before, to):
        buf_part = part(b, q)

        @pl.when(has_before)
        def _():
            rs_copy(buf, way, b, q, to).wait_recv()
            buf[b, rs_rows(q), :] += buf_part

        @pl.when(jnp.logical_not(has_before))
        def _():
            buf[b, rs_rows(q), :] = buf_part

        rs_copy(buf, way, b, q, to).start()

    def rs_both(s, q):
        @pl.when(L - 1 - s > z)
        def _():
            rs_step(up, 0, L - 1 - s, q, has_below, above)

        @pl.when(s < z)
        def _():
            rs_step(down, 1, s, q, has_above, below)

    def rs_stage(s):
        def one(q, _):
            rs_both(s, q)
            return 0
        lax.fori_loop(0, Q, one, 0)

    acc[...] = jnp.zeros_like(acc)
    A[pl.ds(pl.multiple_of(y * S, S), S), :] = a_ref[:, cols(y)]
    w_slot(z, y)[...] = w_ref[:, cols(y)]
    pl.semaphore_wait(barrier, 1 + nx + has_above.astype(jnp.int32) + has_below.astype(jnp.int32))

    g_own(0)
    w_spread(z, y, True, True)
    a_swap(A).start()
    g_from_pair(0)
    w_swap().start()
    if L > 1:
        g_own(1)
    g_rest(0)
    a_swap(A).wait_recv()
    at_end = jnp.logical_or(z == 0, z == L - 1)

    @pl.when(at_end)
    def _():
        rs_stage(0)

    w_copy(z, oy, 0, above).wait_recv()
    w_spread(z, oy, True, True)
    for p in range(1, L):
        g_from_pair(p)
        if p + 1 < L:
            g_own(p + 1)
        g_rest(p)

    @pl.when(jnp.logical_not(at_end))
    def _():
        rs_stage(0)

    attn_block(z)
    for s in range(1, L):
        rs_stage(s)
        w_wave(s)

    other_rows = pl.ds(pl.multiple_of(oy * S, S), S)
    own_rows = pl.ds(pl.multiple_of(y * S, S), S)
    attn_send[...] = acc[other_rows, :].astype(attn_send.dtype)
    attn_back = copy(attn_send, attn_recv, p_ssem.at[2], p_rsem.at[2], pair)
    attn_back.start()
    attn_ref[:, cols(y)] = acc[own_rows, :].astype(attn_ref.dtype)

    def wg_copy(i):
        r = rs_rows(i)
        return copy(wg_send.at[r, :], wg_recv.at[r, :], p_ssem.at[3 + i], p_rsem.at[3 + i], pair)

    def last(i, _):
        half = Q // 2
        q = lax.rem(i + oy * half, Q)
        total = part(z, q)
        acc[rs_rows(0), :] = total

        @pl.when(has_below)
        def _():
            rs_copy(up, 0, z, q, above).wait_recv()
            acc[rs_rows(0), :] += up[z, rs_rows(q), :]

        @pl.when(has_above)
        def _():
            rs_copy(down, 1, z, q, below).wait_recv()
            acc[rs_rows(0), :] += down[z, rs_rows(q), :]

        @pl.when(i < half)
        def _():
            wg_send[rs_rows(i), :] = acc[rs_rows(0), :]
            wg_copy(i).start()

        @pl.when(i >= half)
        def _():
            wg_ref[rs_rows(i - half), cols(y)] = acc[rs_rows(0), :]
        return 0

    lax.fori_loop(0, Q, last, 0)
    attn_back.wait_recv()
    attn_ref[:, cols(oy)] = attn_recv[...]

    def back(i, _):
        wg_copy(i).wait_recv()
        wg_ref[rs_rows(i), cols(oy)] = wg_recv[rs_rows(i), :]
        wg_copy(i).wait_send()
        return 0

    lax.fori_loop(0, Q // 2, back, 0)

    attn_back.wait_send()
    a_swap(A).wait_send()
    w_swap().wait_send()
    for p in range(L):
        g_sent(p)

    def w_sent(b, _):
        for yy in range(2):
            @pl.when(jnp.logical_and(has_above, b <= z))
            def _():
                w_copy(b, yy, 0, above).wait_send()

            @pl.when(jnp.logical_and(has_below, b >= z))
            def _():
                w_copy(b, yy, 1, below).wait_send()

        def chunk(q, _):
            @pl.when(b > z)
            def _():
                rs_copy(up, 0, b, q, above).wait_send()

            @pl.when(b < z)
            def _():
                rs_copy(down, 1, b, q, below).wait_send()
            return 0
        lax.fori_loop(0, Q, chunk, 0)
        return 0

    lax.fori_loop(0, L, w_sent, 0)


def solution(mesh):
    n_dp, n_t = mesh.shape["dp"], mesh.shape["tensor"]
    L, nx = n_dp // 2, n_t // 2

    def body(out_grad, attn_out, o_weight):
        S, C = attn_out.shape
        R = o_weight.shape[0]
        H, FB, K = C // 2, 2 * R, 2 * S
        Q = FB // CHUNK
        dma = pltpu.SemaphoreType.DMA
        bf16, f32 = jnp.bfloat16, jnp.float32
        vmem = pl.BlockSpec(memory_space=pltpu.VMEM)
        return pl.pallas_call(
            functools.partial(kernel, n_dp, n_t),
            out_shape=(jax.ShapeDtypeStruct((S, C), bf16), jax.ShapeDtypeStruct((R, C), f32)),
            in_specs=[vmem] * 3,
            out_specs=(vmem, vmem),
            scratch_shapes=[
                pltpu.VMEM((L, K, FB), bf16),
                pltpu.VMEM((K, H), bf16),
                pltpu.VMEM((L, FB, H), bf16),
                pltpu.VMEM((L, FB, H), f32),
                pltpu.VMEM((L, FB, H), f32),
                pltpu.VMEM((K, H), f32),
                pltpu.VMEM((S, H), bf16),
                pltpu.VMEM((S, H), bf16),
                pltpu.VMEM((R, H), f32),
                pltpu.VMEM((R, H), f32),
                dma((L, 4 * nx - 1)),
                dma((L, 4 * nx - 1)),
                dma((2, n_dp)),
                dma((n_dp,)),
                dma((2, L, Q)),
                dma((2, L, Q)),
                dma((3 + Q // 2,)),
                dma((3 + Q // 2,)),
            ],
            compiler_params=pltpu.CompilerParams(
                collective_id=0, has_side_effects=True, vmem_limit_bytes=60 * 1024 * 1024),
            cost_estimate=pl.CostEstimate(
                flops=4 * K * FB * L * H, bytes_accessed=8 * R * C, transcendentals=0),
        )(out_grad, attn_out, o_weight)

    return jax.shard_map(
        body,
        mesh=mesh,
        in_specs=(P(("dp", "tensor"), None), P("dp", "tensor"), P("dp", "tensor")),
        out_specs=(P("dp", "tensor"), P("dp", "tensor")),
        check_vma=False,
    )
```

time: 466 us -> 294 us (0.63)
  waiting for transfers between devices: 431 us -> 0 us
  Pallas kernels: 0 us -> 289 us
  matrix products: 20.7 us -> 0 us
  between operations: 13.8 us -> 0.65 us
    pallas_call x0 -> x1, Pallas kernels: none -> 289 us  [body(): pl.pallas_call(functools.partial(kernel, n_dp, n_t), out_shape=(jax.Shape...]
    reduce_scatter x1 -> x0, waiting for transfers between devices: 275 us -> none  [body(): lax.psum_scatter(lax.dot_general(gathered, attn_out, (((0,), (0,)), ((),...]
    all_gather x2 -> x0, waiting for transfers between devices: 155 us -> none  [the longest x1 116 us: body(): full_weight = lax.all_gather(o_weight, 'dp', axis=0, tiled=True)]
    dot_general x2 -> x0, matrix products: 20.7 us -> none  [the longest x1 10.6 us: body(): lax.dot_general(gathered, attn_out, (((0,), (0,)), ((), ())), preferred_e...]
  transfers between devices with their start and end apart: 3 -> 0, of which waited for: 3 -> 0; matrix products, arithmetic and copies ran while one was open for 4% -> 0% of each run, Pallas kernels for 0% -> 0%
where the time goes in v1:
time: 294 us
  Pallas kernels  289 us (98%)
  local copies, waits for them, and re-layouts  3.73 us (1%)
    pallas_call x1, Pallas kernels, body(): pl.pallas_call(functools.partial(kernel, n_dp, n_t), out_shape=(jax.Shape...  289 us

profile of v1, /device:TPU:0, one launch (start us, length us, event | category | flops | bytes accessed | tf_op | source)
XLA Modules:
  0.0 293.8 jit_solution(2246210027235037835)
XLA Ops:
  0.6 289.4 %shard_map.50 = (bf16[512,1024]{1,0:T(8,128)(2,1)}, f32[512,1024]{1,0:T(8,128)}) custom-call(bf16[128,4096]{1,0:T(8,128)(2,1)} %g_ref.1, bf16[512,1024]{1,0:T(8,128)(2,1)} %a_ref.1, bf16[512,1024]{1,0:T(8,128)(2,1)} %w_ref.1), custom_call_target="tpu_custom_call" | custom-call | flops 8589934592 | bytes 4194304 | tf_op jit(solution)/shard_map/pallas_call | solution.py:331
  290.1 0.0 copy-start
  290.1 2.4 copy.7
  292.5 0.0 copy-done
  292.5 1.3 copy.8
Async XLA Ops:
  290.1 2.4 copy-start

commit v2 on v1

--- a/solution.py
+++ b/solution.py
@@ -184,20 +184,26 @@
 
         rs_copy(buf, way, b, q, to).start()
 
-    def rs_both(s, q):
-        @pl.when(L - 1 - s > z)
-        def _():
-            rs_step(up, 0, L - 1 - s, q, has_below, above)
-
-        @pl.when(s < z)
-        def _():
-            rs_step(down, 1, s, q, has_above, below)
+    def perm(i):
+        return lax.rem(i + oy * (Q // 2), Q)
+
+    def rs_iter(i):
+        ui, di = i - z, i - (L - 1 - z)
+        uc, dc = jnp.maximum(ui, 0), jnp.maximum(di, 0)
+
+        @pl.when(jnp.logical_and(ui >= 0, ui < (L - 1 - z) * Q))
+        def _():
+            rs_step(up, 0, L - 1 - uc // Q, perm(lax.rem(uc, Q)), has_below, above)
+
+        @pl.when(jnp.logical_and(di >= 0, di < z * Q))
+        def _():
+            rs_step(down, 1, dc // Q, perm(lax.rem(dc, Q)), has_above, below)
 
     def rs_stage(s):
-        def one(q, _):
-            rs_both(s, q)
+        def one(i, _):
+            rs_iter(i)
             return 0
-        lax.fori_loop(0, Q, one, 0)
+        lax.fori_loop(s * Q, (s + 1) * Q, one, 0)
 
     acc[...] = jnp.zeros_like(acc)
     A[pl.ds(pl.multiple_of(y * S, S), S), :] = a_ref[:, cols(y)]
@@ -233,8 +239,9 @@
 
     attn_block(z)
     for s in range(1, L):
-        rs_stage(s)
         w_wave(s)
+        if s < L - 1:
+            rs_stage(s)
 
     other_rows = pl.ds(pl.multiple_of(oy * S, S), S)
     own_rows = pl.ds(pl.multiple_of(y * S, S), S)
@@ -249,7 +256,7 @@
 
     def last(i, _):
         half = Q // 2
-        q = lax.rem(i + oy * half, Q)
+        q = perm(i)
         total = part(z, q)
         acc[rs_rows(0), :] = total
 

time: 294 us -> 224 us (0.76)
  Pallas kernels: 289 us -> 220 us
    pallas_call x1, Pallas kernels: 289 us -> 220 us  [body(): pl.pallas_call(functools.partial(kernel, n_dp, n_t), out_shape=(jax.Shape...]
where the time goes in v2:
time: 224 us
  Pallas kernels  220 us (98%)
  local copies, waits for them, and re-layouts  3.73 us (2%)
    pallas_call x1, Pallas kernels, body(): pl.pallas_call(functools.partial(kernel, n_dp, n_t), out_shape=(jax.Shape...  220 us

profile of v2, /device:TPU:0, one launch (start us, length us, event | category | flops | bytes accessed | tf_op | source)
XLA Modules:
  0.0 224.0 jit_solution(5263111167679430459)
XLA Ops:
  0.6 219.6 %shard_map.50 = (bf16[512,1024]{1,0:T(8,128)(2,1)}, f32[512,1024]{1,0:T(8,128)}) custom-call(bf16[128,4096]{1,0:T(8,128)(2,1)} %g_ref.1, bf16[512,1024]{1,0:T(8,128)(2,1)} %a_ref.1, bf16[512,1024]{1,0:T(8,128)(2,1)} %w_ref.1), custom_call_target="tpu_custom_call" | custom-call | flops 8589934592 | bytes 4194304 | tf_op jit(solution)/shard_map/pallas_call | solution.py:338
  220.3 0.0 copy-start
  220.3 2.4 %copy.7 = bf16[512,1024]{1,0:T(8,128)(2,1)} copy(bf16[512,1024]{1,0:T(8,128)(2,1)} %get-tuple-element.4) | data formatting | bytes 2097152
  222.7 0.0 copy-done
  222.7 1.3 copy.8
Async XLA Ops:
  220.3 2.4 %copy-start = (f32[512,1024]{1,0:T(8,128)S(1)}, f32[512,1024]{1,0:T(8,128)}, u32[]{:S(2)}) copy-start(f32[512,1024]{1,0:T(8,128)} %get-tuple-element.5) | copy-start | bytes 6291460

commit v3 on v2

--- a/solution.py
+++ b/solution.py
@@ -11,7 +11,7 @@
 CHUNK = 256
 
 
-def kernel(n_dp, n_t, g_ref, a_ref, w_ref, attn_ref, wg_ref,
+def sum_kernel(n_dp, n_t, g_ref, a_ref, w_ref, attn_ref, wg_ref,
            G, A, W, up, down, acc, attn_send, attn_recv, wg_send, wg_recv,
            g_ssem, g_rsem, w_ssem, w_rsem, rs_ssem, rs_rsem, p_ssem, p_rsem):
     L, nx = n_dp // 2, n_t // 2
@@ -323,6 +323,364 @@
     lax.fori_loop(0, L, w_sent, 0)
 
 
+def gather_kernel(n_t, g_ref, a_ref, w_ref, attn_ref, wg_ref,
+                  G, GX, A, W, acc, attn_send, attn_recv, far, far_recv, wg_send, wg_recv,
+                  g_ssem, g_rsem, z_ssem, z_rsem, w_ssem, w_rsem, a_ssem, a_rsem,
+                  far_ssem, far_rsem, p_ssem, p_rsem):
+    L, nx = 4, n_t // 2
+    T, S, R = g_ref.shape[0], a_ref.shape[0], w_ref.shape[0]
+    H = a_ref.shape[1] // 2
+    FB = 2 * R
+    Q = FB // CHUNK
+    K = 2 * S
+    half = Q // 2
+    d, t = lax.axis_index("dp"), lax.axis_index("tensor")
+    z, y = d // 2, d % 2
+    x, c = t // 2, t % 2
+    oy = 1 - y
+    pair, core = (d + 1 - 2 * y, t), (d, t + 1 - 2 * c)
+    above, below = (d + 2, t), (d - 2, t)
+    has_above, has_below = z < L - 1, z > 0
+    top = z // 2
+    middle = jnp.logical_or(z == 1, z == 2)
+    at_end = jnp.logical_not(middle)
+
+    def layer(zz):
+        return (zz * 2 + y, t)
+
+    def beside(k):
+        return (d, lax.rem(x + k, nx) * 2 + c)
+
+    def cols(h):
+        return pl.ds(pl.multiple_of(h * H, H), H)
+
+    def copy(src, dst, ssem, rsem, to):
+        return pltpu.make_async_remote_copy(
+            src_ref=src, dst_ref=dst, send_sem=ssem, recv_sem=rsem, device_id=to, device_id_type=MESH)
+
+    barrier = pltpu.get_barrier_semaphore()
+
+    def greet(to):
+        pl.semaphore_signal(barrier, inc=1, device_id=to, device_id_type=MESH)
+
+    for other in [pair, core] + [beside(k) for k in range(1, nx)]:
+        greet(other)
+    pl.when(has_above)(lambda: greet(above))
+    pl.when(has_below)(lambda: greet(below))
+    pl.when(z < 2)(lambda: greet((d + 4, t)))
+    pl.when(z >= 2)(lambda: greet((d - 4, t)))
+
+    def g_slot(p, yy, xx, cc):
+        return G.at[p, pl.ds(pl.multiple_of((yy * n_t + xx * 2 + cc) * T, T), T), :]
+
+    def gx_slot(p, yy, xx, cc):
+        return GX.at[p - L, pl.ds(pl.multiple_of((yy * n_t + xx * 2 + cc) * T, T), T), :]
+
+    def g_copy(p, slot, s_idx, r_idx, to):
+        return copy(slot, slot, g_ssem.at[p, s_idx], g_rsem.at[p, r_idx], to)
+
+    def xm(m):
+        return lax.rem(x + m, nx)
+
+    def to_core(p, slot, j):
+        g_copy(p, slot, 2 * nx - 1 + j, 2 * nx - 1 + j, core).start()
+
+    def spread(p, at):
+        slot = at(p, y, x, c)
+        g_copy(p, slot, 0, 0, pair).start()
+        for k in range(1, nx):
+            g_copy(p, slot, k, nx - k, beside(k)).start()
+        to_core(p, slot, 0)
+
+    def arrived(p, slot, r_idx):
+        g_copy(p, slot, r_idx, r_idx, core).wait_recv()
+
+    def from_pair(p, at):
+        slot = at(p, oy, x, c)
+        arrived(p, slot, 0)
+        for k in range(1, nx):
+            g_copy(p, slot, nx - 1 + k, nx - 1 + nx - k, beside(k)).start()
+        to_core(p, slot, nx)
+
+    def rest(p, at):
+        for m in range(1, nx):
+            slot = at(p, y, xm(m), c)
+            arrived(p, slot, m)
+            to_core(p, slot, m)
+        for m in range(1, nx):
+            slot = at(p, oy, xm(m), c)
+            arrived(p, slot, nx - 1 + m)
+            to_core(p, slot, nx + m)
+        for yy in range(2):
+            for m in range(nx):
+                arrived(p, at(p, y if yy == 0 else oy, xm(m), 1 - c), 2 * nx - 1 + yy * nx + m)
+
+    def all_sent(p, at):
+        for i in range(4 * nx - 1):
+            g_copy(p, at(p, y, x, c), i, i, core).wait_send()
+
+    def z_copy(h, j):
+        return copy(g_slot(2 * h + j, y, x, c), gx_slot(L + z * 2 + j, y, x, c),
+                    z_ssem.at[h * 2 + j], z_rsem.at[z * 2 + j], layer(1 + h))
+
+    def z_all(act):
+        for h in (0, 1):
+            @pl.when(z != 1 + h)
+            def _():
+                for j in (0, 1):
+                    act(z_copy(h, j))
+
+    def extra_layer(e):
+        o = jnp.where(e == 0, 0, e + 1)
+        return jnp.where(z == 1, o, L - 1 - o)
+
+    def z_arrived(zz, j):
+        p = L + zz * 2 + j
+        slot = gx_slot(p, y, x, c)
+        copy(slot, slot, z_ssem.at[0], z_rsem.at[zz * 2 + j], core).wait_recv()
+        spread(p, gx_slot)
+
+    def extra(e):
+        zz = extra_layer(e)
+        for j in (0, 1):
+            from_pair(L + zz * 2 + j, gx_slot)
+            rest(L + zz * 2 + j, gx_slot)
+
+    def unit(buf, b, yy, size):
+        return buf.at[b, pl.ds(pl.multiple_of(yy * size, size), size), :]
+
+    def w_copy(b, yy, way, to):
+        slot = unit(W, b, yy, R)
+        return copy(slot, slot, w_ssem.at[way, b * 2 + yy], w_rsem.at[b * 2 + yy], to)
+
+    def a_copy(b, yy, way, to):
+        slot = unit(A, b, yy, S)
+        return copy(slot, slot, a_ssem.at[way, b * 2 + yy], a_rsem.at[b * 2 + yy], to)
+
+    def a_up(b):
+        return jnp.logical_and(z <= 1, b <= z)
+
+    def a_down(b):
+        return jnp.logical_and(z >= 2, b >= z)
+
+    def a_spread(b, yy):
+        pl.when(a_up(b))(lambda: a_copy(b, yy, 0, above).start())
+        pl.when(a_down(b))(lambda: a_copy(b, yy, 1, below).start())
+
+    def w_out(b, yy):
+        pl.when(jnp.logical_and(z == 2, b <= z))(lambda: w_copy(b, yy, 0, above).start())
+        pl.when(jnp.logical_and(z == 1, b >= z))(lambda: w_copy(b, yy, 1, below).start())
+
+    def w_in(b, yy):
+        pl.when(jnp.logical_and(z <= 1, b <= z))(lambda: w_copy(b, yy, 0, above).start())
+        pl.when(jnp.logical_and(z >= 2, b >= z))(lambda: w_copy(b, yy, 1, below).start())
+
+    def a_swap():
+        return copy(a_ref.at[:, cols(oy)], unit(A, z, y, S), p_ssem.at[0], a_rsem.at[d], pair)
+
+    def w_swap():
+        return copy(w_ref.at[:, cols(oy)], unit(W, z, y, R), p_ssem.at[1], w_rsem.at[d], pair)
+
+    def attn_block(b):
+        def rows(i, _):
+            r = pl.ds(pl.multiple_of(i * 256, 256), 256)
+            acc[r, :] += jnp.dot(G[b, r, :], W[b], preferred_element_type=jnp.float32)
+            return 0
+        lax.fori_loop(0, K // 256, rows, 0)
+
+    def w_wave(h):
+        for b, ok in ((z - h, z - h >= 0), (z + h, z + h <= L - 1)):
+            @pl.when(ok)
+            def _():
+                for yy in range(2):
+                    w_copy(b, yy, 0, core).wait_recv()
+                    pl.when(jnp.logical_and(has_above, b < z))(lambda: w_copy(b, yy, 0, above).start())
+                    pl.when(jnp.logical_and(has_below, b > z))(lambda: w_copy(b, yy, 1, below).start())
+        for b, ok in ((z - h, z - h >= 0), (z + h, z + h <= L - 1)):
+            pl.when(ok)(lambda: attn_block(b))
+
+    def a_wave(b):
+        for yy in range(2):
+            a_copy(b, yy, 0, core).wait_recv()
+            a_spread(b, yy)
+
+    def q_rows(q):
+        return pl.ds(pl.multiple_of(q * CHUNK, CHUNK), CHUNK)
+
+    def perm(i):
+        return lax.rem(i + oy * half, Q)
+
+    def part(g, a):
+        return lax.dot_general(g, a, (((0,), (0,)), ((), ())), preferred_element_type=jnp.float32)
+
+    def rows_of(b, q):
+        total = part(G[b, :, q_rows(q)], A[z])
+        for e in range(3):
+            zz = extra_layer(e)
+            total += part(GX[zz * 2 + b - 2 * top, :, q_rows(q)], A[zz])
+        return total
+
+    def far_copy(q):
+        return copy(far.at[q_rows(q), :], far_recv.at[q_rows(q), :], far_ssem.at[q], far_rsem.at[q], layer(3 * top))
+
+    def far_landed(q):
+        return copy(far.at[q_rows(q), :], far_recv.at[q_rows(q), :], far_ssem.at[q], far_rsem.at[q], core)
+
+    def make_far(i, _):
+        q = perm(i)
+        far[q_rows(q), :] = rows_of(3 * top, q)
+        far_copy(q).start()
+        return 0
+
+    def wg_copy(src, i):
+        return copy(src, wg_recv.at[q_rows(i), :], p_ssem.at[3 + i], p_rsem.at[3 + i], pair)
+
+    def make_near(i, _):
+        value = rows_of(z, perm(i))
+
+        @pl.when(i < half)
+        def _():
+            wg_send[q_rows(i), :] = value
+            wg_copy(wg_send.at[q_rows(i), :], i).start()
+
+        @pl.when(i >= half)
+        def _():
+            wg_ref[q_rows(i - half), cols(y)] = value
+        return 0
+
+    def take_far(i, _):
+        q = perm(i)
+        far_landed(q).wait_recv()
+
+        @pl.when(i < half)
+        def _():
+            wg_copy(far_recv.at[q_rows(q), :], i).start()
+
+        @pl.when(i >= half)
+        def _():
+            wg_ref[q_rows(i - half), cols(y)] = far_recv[q_rows(q), :]
+        return 0
+
+    order = [L - 1, 0, L - 2, 1]
+    for p in range(L):
+        g_slot(p, y, x, c)[...] = g_ref[:, p * FB:(p + 1) * FB]
+    unit(A, z, y, S)[...] = a_ref[:, cols(y)]
+    unit(W, z, y, R)[...] = w_ref[:, cols(y)]
+    pl.semaphore_wait(barrier, 2 + nx + has_above.astype(jnp.int32) + has_below.astype(jnp.int32))
+
+    a_swap().start()
+    z_all(lambda cp: cp.start())
+    spread(order[0], g_slot)
+    a_spread(z, y)
+    w_swap().start()
+    w_out(z, y)
+    from_pair(order[0], g_slot)
+    spread(order[1], g_slot)
+    rest(order[0], g_slot)
+    a_copy(z, oy, 0, core).wait_recv()
+    a_spread(z, oy)
+    w_copy(z, oy, 0, core).wait_recv()
+    w_out(z, oy)
+
+    @pl.when(at_end)
+    def _():
+        for yy in range(2):
+            w_in(z, yy)
+
+    @pl.when(middle)
+    def _():
+        for j in (0, 1):
+            z_arrived(extra_layer(0), j)
+        a_wave(extra_layer(0))
+        for yy in range(2):
+            w_in(z, yy)
+
+    for i in range(1, L):
+        from_pair(order[i], g_slot)
+        if i + 1 < L:
+            spread(order[i + 1], g_slot)
+        rest(order[i], g_slot)
+
+    @pl.when(middle)
+    def _():
+        for j in (0, 1):
+            z_arrived(extra_layer(1), j)
+        extra(0)
+        for j in (0, 1):
+            z_arrived(extra_layer(2), j)
+        extra(1)
+
+    acc[...] = jnp.zeros_like(acc)
+    attn_block(z)
+    w_wave(1)
+
+    @pl.when(middle)
+    def _():
+        a_wave(extra_layer(1))
+        extra(2)
+        a_wave(extra_layer(2))
+        lax.fori_loop(0, Q, make_far, 0)
+
+    w_wave(2)
+
+    @pl.when(middle)
+    def _():
+        lax.fori_loop(0, Q, make_near, 0)
+
+    w_wave(3)
+
+    attn_send[...] = acc[pl.ds(pl.multiple_of(oy * S, S), S), :].astype(attn_send.dtype)
+    attn_back = copy(attn_send, attn_recv, p_ssem.at[2], p_rsem.at[2], pair)
+    attn_back.start()
+    attn_ref[:, cols(y)] = acc[pl.ds(pl.multiple_of(y * S, S), S), :].astype(attn_ref.dtype)
+
+    @pl.when(at_end)
+    def _():
+        lax.fori_loop(0, Q, take_far, 0)
+
+    attn_back.wait_recv()
+    attn_ref[:, cols(oy)] = attn_recv[...]
+
+    def back(i, _):
+        cp = wg_copy(wg_send.at[q_rows(i), :], i)
+        cp.wait_recv()
+        wg_ref[q_rows(i), cols(oy)] = wg_recv[q_rows(i), :]
+        cp.wait_send()
+        return 0
+
+    lax.fori_loop(0, half, back, 0)
+
+    attn_back.wait_send()
+    a_swap().wait_send()
+    w_swap().wait_send()
+    z_all(lambda cp: cp.wait_send())
+    for p in range(L):
+        all_sent(p, g_slot)
+
+    @pl.when(middle)
+    def _():
+        def sent(e, _):
+            zz = extra_layer(e // 2)
+            all_sent(L + zz * 2 + e % 2, gx_slot)
+            return 0
+        lax.fori_loop(0, 6, sent, 0)
+
+        def far_sent(q, _):
+            far_copy(q).wait_send()
+            return 0
+        lax.fori_loop(0, Q, far_sent, 0)
+
+    def line_sent(b, _):
+        for yy in range(2):
+            pl.when(jnp.logical_and(has_above, b <= z))(lambda: w_copy(b, yy, 0, above).wait_send())
+            pl.when(jnp.logical_and(has_below, b >= z))(lambda: w_copy(b, yy, 1, below).wait_send())
+            pl.when(a_up(b))(lambda: a_copy(b, yy, 0, above).wait_send())
+            pl.when(a_down(b))(lambda: a_copy(b, yy, 1, below).wait_send())
+        return 0
+
+    lax.fori_loop(0, L, line_sent, 0)
+
+
 def solution(mesh):
     n_dp, n_t = mesh.shape["dp"], mesh.shape["tensor"]
     L, nx = n_dp // 2, n_t // 2
@@ -335,12 +693,46 @@
         dma = pltpu.SemaphoreType.DMA
         bf16, f32 = jnp.bfloat16, jnp.float32
         vmem = pl.BlockSpec(memory_space=pltpu.VMEM)
-        return pl.pallas_call(
-            functools.partial(kernel, n_dp, n_t),
-            out_shape=(jax.ShapeDtypeStruct((S, C), bf16), jax.ShapeDtypeStruct((R, C), f32)),
-            in_specs=[vmem] * 3,
-            out_specs=(vmem, vmem),
-            scratch_shapes=[
+        def call(body_of, scratch, collective_id):
+            return pl.pallas_call(
+                body_of,
+                out_shape=(jax.ShapeDtypeStruct((S, C), bf16), jax.ShapeDtypeStruct((R, C), f32)),
+                in_specs=[vmem] * 3,
+                out_specs=(vmem, vmem),
+                scratch_shapes=scratch,
+                compiler_params=pltpu.CompilerParams(
+                    collective_id=collective_id, has_side_effects=True, vmem_limit_bytes=60 * 1024 * 1024),
+                cost_estimate=pl.CostEstimate(
+                    flops=4 * K * FB * L * H, bytes_accessed=8 * R * C, transcendentals=0),
+            )(out_grad, attn_out, o_weight)
+
+        if L == 4 and 2 * K * FB * (L + 2 * L) <= 32 * 1024 * 1024:
+            return call(functools.partial(gather_kernel, n_t), [
+                pltpu.VMEM((L, K, FB), bf16),
+                pltpu.VMEM((2 * L, K, FB), bf16),
+                pltpu.VMEM((L, K, H), bf16),
+                pltpu.VMEM((L, FB, H), bf16),
+                pltpu.VMEM((K, H), f32),
+                pltpu.VMEM((S, H), bf16),
+                pltpu.VMEM((S, H), bf16),
+                pltpu.VMEM((FB, H), f32),
+                pltpu.VMEM((FB, H), f32),
+                pltpu.VMEM((R, H), f32),
+                pltpu.VMEM((R, H), f32),
+                dma((3 * L, 4 * nx - 1)),
+                dma((3 * L, 4 * nx - 1)),
+                dma((4,)),
+                dma((2 * L,)),
+                dma((2, n_dp)),
+                dma((n_dp,)),
+                dma((2, n_dp)),
+                dma((n_dp,)),
+                dma((Q,)),
+                dma((Q,)),
+                dma((3 + Q // 2,)),
+                dma((3 + Q // 2,)),
+            ], 1)
+        return call(functools.partial(sum_kernel, n_dp, n_t), [
                 pltpu.VMEM((L, K, FB), bf16),
                 pltpu.VMEM((K, H), bf16),
                 pltpu.VMEM((L, FB, H), bf16),
@@ -359,12 +751,7 @@
                 dma((2, L, Q)),
                 dma((3 + Q // 2,)),
                 dma((3 + Q // 2,)),
-            ],
-            compiler_params=pltpu.CompilerParams(
-                collective_id=0, has_side_effects=True, vmem_limit_bytes=60 * 1024 * 1024),
-            cost_estimate=pl.CostEstimate(
-                flops=4 * K * FB * L * H, bytes_accessed=8 * R * C, transcendentals=0),
-        )(out_grad, attn_out, o_weight)
+        ], 0)
 
     return jax.shard_map(
         body,

time: 224 us -> 282 us (1.26)
  Pallas kernels: 220 us -> 277 us
    pallas_call x1, Pallas kernels: 220 us -> 277 us  [call(): pl.pallas_call(body_of, out_shape=(jax.ShapeDtypeStruct((S, C), bf16), ja...]
where the time goes in v3:
time: 282 us; the launch traced here: 281 us
  Pallas kernels  277 us (98%)
  local copies, waits for them, and re-layouts  3.73 us (1%)
    pallas_call x1, Pallas kernels, call(): pl.pallas_call(body_of, out_shape=(jax.ShapeDtypeStruct((S, C), bf16), ja...  277 us

profile of v3, /device:TPU:0, one launch (start us, length us, event | category | flops | bytes accessed | tf_op | source)
XLA Modules:
  0.0 281.4 jit_solution(3662659486963822471)
XLA Ops:
  0.6 277.1 %shard_map.50 = (bf16[512,1024]{1,0:T(8,128)(2,1)}, f32[512,1024]{1,0:T(8,128)}) custom-call(bf16[128,4096]{1,0:T(8,128)(2,1)} %g_ref.1, bf16[512,1024]{1,0:T(8,128)(2,1)} %a_ref.1, bf16[512,1024]{1,0:T(8,128)(2,1)} %w_ref.1), custom_call_target="tpu_custom_call" | custom-call | flops 8589934592 | bytes 4194304 | tf_op jit(solution)/shard_map/pallas_call | solution.py:697
  277.7 0.0 copy-start
  277.7 2.4 copy.7
  280.1 0.0 copy-done
  280.1 1.3 copy.8
Async XLA Ops:
  277.7 2.4 copy-start

commit v4 on v2

--- a/solution.py
+++ b/solution.py
@@ -151,6 +151,7 @@
                 w_copy(z + h, yy, 1, below).wait_recv()
                 w_spread(z + h, yy, False, True)
 
+    def attn_wave(h):
         @pl.when(z - h >= 0)
         def _():
             attn_block(z - h)
@@ -210,13 +211,13 @@
     w_slot(z, y)[...] = w_ref[:, cols(y)]
     pl.semaphore_wait(barrier, 1 + nx + has_above.astype(jnp.int32) + has_below.astype(jnp.int32))
 
+    a_swap(A).start()
     g_own(0)
     w_spread(z, y, True, True)
-    a_swap(A).start()
     g_from_pair(0)
     w_swap().start()
-    if L > 1:
-        g_own(1)
+    for p in range(1, min(L, 3)):
+        g_own(p)
     g_rest(0)
     a_swap(A).wait_recv()
     at_end = jnp.logical_or(z == 0, z == L - 1)
@@ -225,23 +226,28 @@
     def _():
         rs_stage(0)
 
+    if L > 1:
+        g_from_pair(1)
     w_copy(z, oy, 0, above).wait_recv()
     w_spread(z, oy, True, True)
+    for p in range(3, L):
+        g_own(p)
+    for p in range(2, L):
+        g_from_pair(p)
     for p in range(1, L):
-        g_from_pair(p)
-        if p + 1 < L:
-            g_own(p + 1)
         g_rest(p)
 
     @pl.when(jnp.logical_not(at_end))
     def _():
         rs_stage(0)
 
-    attn_block(z)
     for s in range(1, L):
         w_wave(s)
         if s < L - 1:
             rs_stage(s)
+        if s == 1:
+            attn_block(z)
+        attn_wave(s)
 
     other_rows = pl.ds(pl.multiple_of(oy * S, S), S)
     own_rows = pl.ds(pl.multiple_of(y * S, S), S)

time: 224 us -> 219 us (0.978)
  Pallas kernels: 220 us -> 214 us
    pallas_call x1, Pallas kernels: 220 us -> 214 us  [body(): pl.pallas_call(functools.partial(kernel, n_dp, n_t), out_shape=(jax.Shape...]
where the time goes in v4:
time: 219 us
  Pallas kernels  214 us (98%)
  local copies, waits for them, and re-layouts  3.73 us (2%)
    pallas_call x1, Pallas kernels, body(): pl.pallas_call(functools.partial(kernel, n_dp, n_t), out_shape=(jax.Shape...  214 us

profile of v4, /device:TPU:0, one launch (start us, length us, event | category | flops | bytes accessed | tf_op | source)
XLA Modules:
  0.0 218.7 jit_solution(11525081195517450296)
XLA Ops:
  0.6 214.3 %shard_map.50 = (bf16[512,1024]{1,0:T(8,128)(2,1)}, f32[512,1024]{1,0:T(8,128)}) custom-call(bf16[128,4096]{1,0:T(8,128)(2,1)} %g_ref.1, bf16[512,1024]{1,0:T(8,128)(2,1)} %a_ref.1, bf16[512,1024]{1,0:T(8,128)(2,1)} %w_ref.1), custom_call_target="tpu_custom_call" | custom-call | flops 8589934592 | bytes 4194304 | tf_op jit(solution)/shard_map/pallas_call | solution.py:344
  215.0 0.0 copy-start
  215.0 2.4 %copy.7 = bf16[512,1024]{1,0:T(8,128)(2,1)} copy(bf16[512,1024]{1,0:T(8,128)(2,1)} %get-tuple-element.4) | data formatting | bytes 2097152
  217.4 0.0 copy-done
  217.4 1.3 copy.8
Async XLA Ops:
  215.0 2.4 %copy-start = (f32[512,1024]{1,0:T(8,128)S(1)}, f32[512,1024]{1,0:T(8,128)}, u32[]{:S(2)}) copy-start(f32[512,1024]{1,0:T(8,128)} %get-tuple-element.5) | copy-start | bytes 6291460

commit v5 on v4

--- a/solution.py
+++ b/solution.py
@@ -13,7 +13,7 @@
 
 def kernel(n_dp, n_t, g_ref, a_ref, w_ref, attn_ref, wg_ref,
            G, A, W, up, down, acc, attn_send, attn_recv, wg_send, wg_recv,
-           g_ssem, g_rsem, w_ssem, w_rsem, rs_ssem, rs_rsem, p_ssem, p_rsem):
+           g_ssem, g_rsem, w_ssem, w_rsem, rs_ssem, rs_rsem, p_ssem, p_rsem, e_ssem, e_rsem):
     L, nx = n_dp // 2, n_t // 2
     T, S, R = g_ref.shape[0], a_ref.shape[0], w_ref.shape[0]
     H = a_ref.shape[1] // 2
@@ -27,6 +27,12 @@
     pair, core = (d + 1 - 2 * y, t), (d, t + 1 - 2 * c)
     above, below = (d + 2, t), (d - 2, t)
     has_above, has_below = z < L - 1, z > 0
+    at_end = jnp.logical_or(z == 0, z == L - 1)
+    by_low, by_high = z == 1, z == L - 2
+    by_end = jnp.logical_or(by_low, by_high)
+    neighbour = (jnp.where(z == 0, d + 2, d - 2), t)
+    sums_up = jnp.where(z == 0, L - 2, L - 1 - z)
+    sums_down = jnp.where(z == L - 1, L - 2, z)
 
     def beside(k):
         return (d, lax.rem(x + k, nx) * 2 + c)
@@ -53,6 +59,8 @@
     order = [v for s in range((L + 1) // 2) for v in ([L - 1 - s, s] if s != L - 1 - s else [s])]
 
     def block_at(p):
+        if p == L:
+            return L
         return jnp.where(z < (L + 1) // 2, order[p], L - 1 - order[p])
 
     def g_slot(b, yy, xx, cc):
@@ -69,6 +77,9 @@
         b = block_at(p)
         slot = g_slot(b, y, x, c)
         slot[...] = g_ref[:, pl.ds(pl.multiple_of(b * FB, FB), FB)]
+        g_spread(p, slot)
+
+    def g_spread(p, slot):
         g_copy(p, slot, 0, 0, pair).start()
         for k in range(1, nx):
             g_copy(p, slot, k, nx - k, beside(k)).start()
@@ -124,9 +135,22 @@
             def _():
                 w_copy(b, yy, 1, below).start()
 
-    def a_swap(buf):
-        return copy(a_ref.at[:, cols(oy)], buf.at[pl.ds(pl.multiple_of(y * S, S), S), :],
+    def a_slot(i, yy):
+        return A.at[i, pl.ds(pl.multiple_of(yy * S, S), S), :]
+
+    def a_swap():
+        return copy(a_ref.at[:, cols(oy)], a_slot(0, y),
                     p_ssem.at[0], p_rsem.at[0], pair)
+
+    def end_copy(i):
+        if i == 2:
+            b = jnp.where(z == 0, 1, L - 2)
+            src = g_ref.at[:, pl.ds(pl.multiple_of(b * FB, FB), FB)]
+            dst = g_slot(L, y, x, c)
+        else:
+            yy = y if i == 0 else oy
+            src, dst = a_slot(0, yy), a_slot(1, yy)
+        return copy(src, dst, e_ssem.at[i], e_rsem.at[i], neighbour)
 
     def w_swap():
         return copy(w_ref.at[:, cols(oy)], w_slot(z, y), p_ssem.at[1], w_rsem.at[d], pair)
@@ -167,8 +191,8 @@
         slot = buf.at[b, rs_rows(q), :]
         return copy(slot, slot, rs_ssem.at[way, b, q], rs_rsem.at[way, b, q], to)
 
-    def part(b, q):
-        return lax.dot_general(G[b, :, rs_rows(q)], A[...], (((0,), (0,)), ((), ())),
+    def part(b, q, i=0):
+        return lax.dot_general(G[b, :, rs_rows(q)], A[i], (((0,), (0,)), ((), ())),
                                preferred_element_type=jnp.float32)
 
     def rs_step(buf, way, b, q, has_before, to):
@@ -192,11 +216,11 @@
         ui, di = i - z, i - (L - 1 - z)
         uc, dc = jnp.maximum(ui, 0), jnp.maximum(di, 0)
 
-        @pl.when(jnp.logical_and(ui >= 0, ui < (L - 1 - z) * Q))
+        @pl.when(jnp.logical_and(ui >= 0, ui < sums_up * Q))
         def _():
             rs_step(up, 0, L - 1 - uc // Q, perm(lax.rem(uc, Q)), has_below, above)
 
-        @pl.when(jnp.logical_and(di >= 0, di < z * Q))
+        @pl.when(jnp.logical_and(di >= 0, di < sums_down * Q))
         def _():
             rs_step(down, 1, dc // Q, perm(lax.rem(dc, Q)), has_above, below)
 
@@ -207,24 +231,30 @@
         lax.fori_loop(s * Q, (s + 1) * Q, one, 0)
 
     acc[...] = jnp.zeros_like(acc)
-    A[pl.ds(pl.multiple_of(y * S, S), S), :] = a_ref[:, cols(y)]
+    a_slot(0, y)[...] = a_ref[:, cols(y)]
     w_slot(z, y)[...] = w_ref[:, cols(y)]
     pl.semaphore_wait(barrier, 1 + nx + has_above.astype(jnp.int32) + has_below.astype(jnp.int32))
 
-    a_swap(A).start()
+    a_swap().start()
     g_own(0)
     w_spread(z, y, True, True)
+
+    @pl.when(at_end)
+    def _():
+        end_copy(2).start()
+        end_copy(0).start()
+
     g_from_pair(0)
     w_swap().start()
     for p in range(1, min(L, 3)):
         g_own(p)
     g_rest(0)
-    a_swap(A).wait_recv()
-    at_end = jnp.logical_or(z == 0, z == L - 1)
+    a_swap().wait_recv()
 
     @pl.when(at_end)
     def _():
         rs_stage(0)
+        end_copy(1).start()
 
     if L > 1:
         g_from_pair(1)
@@ -234,12 +264,26 @@
         g_own(p)
     for p in range(2, L):
         g_from_pair(p)
+
+    @pl.when(by_end)
+    def _():
+        end_copy(2).wait_recv()
+        g_spread(L, g_slot(L, y, x, c))
+
     for p in range(1, L):
         g_rest(p)
 
+    @pl.when(by_end)
+    def _():
+        g_from_pair(L)
+
     @pl.when(jnp.logical_not(at_end))
     def _():
         rs_stage(0)
+
+    @pl.when(by_end)
+    def _():
+        g_rest(L)
 
     for s in range(1, L):
         w_wave(s)
@@ -266,12 +310,16 @@
         total = part(z, q)
         acc[rs_rows(0), :] = total
 
-        @pl.when(has_below)
+        @pl.when(by_end)
+        def _():
+            acc[rs_rows(0), :] += part(L, q, 1)
+
+        @pl.when(jnp.logical_and(has_below, jnp.logical_not(by_low)))
         def _():
             rs_copy(up, 0, z, q, above).wait_recv()
             acc[rs_rows(0), :] += up[z, rs_rows(q), :]
 
-        @pl.when(has_above)
+        @pl.when(jnp.logical_and(has_above, jnp.logical_not(by_high)))
         def _():
             rs_copy(down, 1, z, q, below).wait_recv()
             acc[rs_rows(0), :] += down[z, rs_rows(q), :]
@@ -285,6 +333,11 @@
         def _():
             wg_ref[rs_rows(i - half), cols(y)] = acc[rs_rows(0), :]
         return 0
+
+    @pl.when(by_end)
+    def _():
+        end_copy(0).wait_recv()
+        end_copy(1).wait_recv()
 
     lax.fori_loop(0, Q, last, 0)
     attn_back.wait_recv()
@@ -299,11 +352,20 @@
     lax.fori_loop(0, Q // 2, back, 0)
 
     attn_back.wait_send()
-    a_swap(A).wait_send()
+    a_swap().wait_send()
     w_swap().wait_send()
     for p in range(L):
         g_sent(p)
 
+    @pl.when(by_end)
+    def _():
+        g_sent(L)
+
+    @pl.when(at_end)
+    def _():
+        for i in range(3):
+            end_copy(i).wait_send()
+
     def w_sent(b, _):
         for yy in range(2):
             @pl.when(jnp.logical_and(has_above, b <= z))
@@ -315,11 +377,11 @@
                 w_copy(b, yy, 1, below).wait_send()
 
         def chunk(q, _):
-            @pl.when(b > z)
+            @pl.when(b >= L - sums_up)
             def _():
                 rs_copy(up, 0, b, q, above).wait_send()
 
-            @pl.when(b < z)
+            @pl.when(b < sums_down)
             def _():
                 rs_copy(down, 1, b, q, below).wait_send()
             return 0
@@ -347,8 +409,8 @@
             in_specs=[vmem] * 3,
             out_specs=(vmem, vmem),
             scratch_shapes=[
-                pltpu.VMEM((L, K, FB), bf16),
-                pltpu.VMEM((K, H), bf16),
+                pltpu.VMEM((L + 1, K, FB), bf16),
+                pltpu.VMEM((2, K, H), bf16),
                 pltpu.VMEM((L, FB, H), bf16),
                 pltpu.VMEM((L, FB, H), f32),
                 pltpu.VMEM((L, FB, H), f32),
@@ -357,14 +419,16 @@
                 pltpu.VMEM((S, H), bf16),
                 pltpu.VMEM((R, H), f32),
                 pltpu.VMEM((R, H), f32),
-                dma((L, 4 * nx - 1)),
-                dma((L, 4 * nx - 1)),
+                dma((L + 1, 4 * nx - 1)),
+                dma((L + 1, 4 * nx - 1)),
                 dma((2, n_dp)),
                 dma((n_dp,)),
                 dma((2, L, Q)),
                 dma((2, L, Q)),
                 dma((3 + Q // 2,)),
                 dma((3 + Q // 2,)),
+                dma((3,)),
+                dma((3,)),
             ],
             compiler_params=pltpu.CompilerParams(
                 collective_id=0, has_side_effects=True, vmem_limit_bytes=60 * 1024 * 1024),

time: 219 us -> 221 us (level)
  Pallas kernels: 214 us -> 217 us
    pallas_call x1, Pallas kernels: 214 us -> 217 us  [body(): pl.pallas_call(functools.partial(kernel, n_dp, n_t), out_shape=(jax.Shape...]
where the time goes in v5:
time: 221 us
  Pallas kernels  217 us (98%)
  local copies, waits for them, and re-layouts  3.73 us (2%)
    pallas_call x1, Pallas kernels, body(): pl.pallas_call(functools.partial(kernel, n_dp, n_t), out_shape=(jax.Shape...  217 us

profile of v5, /device:TPU:0, one launch (start us, length us, event | category | flops | bytes accessed | tf_op | source)
XLA Modules:
  0.0 221.1 jit_solution(16424448002436914197)
XLA Ops:
  0.6 216.7 %shard_map.50 = (bf16[512,1024]{1,0:T(8,128)(2,1)}, f32[512,1024]{1,0:T(8,128)}) custom-call(bf16[128,4096]{1,0:T(8,128)(2,1)} %g_ref.1, bf16[512,1024]{1,0:T(8,128)(2,1)} %a_ref.1, bf16[512,1024]{1,0:T(8,128)(2,1)} %w_ref.1), custom_call_target="tpu_custom_call" | custom-call | flops 8589934592 | bytes 4194304 | tf_op jit(solution)/shard_map/pallas_call | solution.py:406
  217.3 0.0 copy-start
  217.4 2.4 %copy.7 = bf16[512,1024]{1,0:T(8,128)(2,1)} copy(bf16[512,1024]{1,0:T(8,128)(2,1)} %get-tuple-element.4) | data formatting | bytes 2097152
  219.8 0.0 copy-done
  219.8 1.3 copy.8
Async XLA Ops:
  217.3 2.4 %copy-start = (f32[512,1024]{1,0:T(8,128)S(1)}, f32[512,1024]{1,0:T(8,128)}, u32[]{:S(2)}) copy-start(f32[512,1024]{1,0:T(8,128)} %get-tuple-element.5) | copy-start | bytes 6291460

commit v6 on v4

--- a/solution.py
+++ b/solution.py
@@ -237,17 +237,32 @@
     for p in range(1, L):
         g_rest(p)
 
+    if L > 1:
+        w_wave(1)
+
+    @pl.when(at_end)
+    def _():
+        for s in range(1, L - 1):
+            rs_stage(s)
+
     @pl.when(jnp.logical_not(at_end))
     def _():
         rs_stage(0)
 
-    for s in range(1, L):
+    for s in range(2, L):
         w_wave(s)
-        if s < L - 1:
-            rs_stage(s)
-        if s == 1:
+
+        @pl.when(jnp.logical_not(at_end))
+        def _():
+            rs_stage(s - 1)
+
+        if s == 2:
             attn_block(z)
-        attn_wave(s)
+        attn_wave(s - 1)
+    if L <= 2:
+        attn_block(z)
+    if L > 1:
+        attn_wave(L - 1)
 
     other_rows = pl.ds(pl.multiple_of(oy * S, S), S)
     own_rows = pl.ds(pl.multiple_of(y * S, S), S)

time: 219 us -> 221 us (level)
  no operation moved by 1% of the time
where the time goes in v6:
time: 221 us; the launch traced here: 220 us
  Pallas kernels  215 us (97%)
  local copies, waits for them, and re-layouts  3.73 us (2%)
    pallas_call x1, Pallas kernels, body(): pl.pallas_call(functools.partial(kernel, n_dp, n_t), out_shape=(jax.Shape...  215 us

profile of v6, /device:TPU:0, one launch (start us, length us, event | category | flops | bytes accessed | tf_op | source)
XLA Modules:
  0.0 219.8 jit_solution(6535527325034854165)
XLA Ops:
  0.6 215.5 %shard_map.50 = (bf16[512,1024]{1,0:T(8,128)(2,1)}, f32[512,1024]{1,0:T(8,128)}) custom-call(bf16[128,4096]{1,0:T(8,128)(2,1)} %g_ref.1, bf16[512,1024]{1,0:T(8,128)(2,1)} %a_ref.1, bf16[512,1024]{1,0:T(8,128)(2,1)} %w_ref.1), custom_call_target="tpu_custom_call" | custom-call | flops 8589934592 | bytes 4194304 | tf_op jit(solution)/shard_map/pallas_call | solution.py:359
  216.1 0.0 copy-start
  216.1 2.4 %copy.7 = bf16[512,1024]{1,0:T(8,128)(2,1)} copy(bf16[512,1024]{1,0:T(8,128)(2,1)} %get-tuple-element.4) | data formatting | bytes 2097152
  218.5 0.0 copy-done
  218.5 1.3 copy.8
Async XLA Ops:
  216.1 2.4 %copy-start = (f32[512,1024]{1,0:T(8,128)S(1)}, f32[512,1024]{1,0:T(8,128)}, u32[]{:S(2)}) copy-start(f32[512,1024]{1,0:T(8,128)} %get-tuple-element.5) | copy-start | bytes 6291460
